TPU v7x, 32 devices: a whole 2x2x4 slice. The times are simulated.
32 devices in a mesh: upd: 4 (over x, core), col: 8 (over z, y).
Axes of the slice: x: 2, y: 2, z: 4, core: 2. Of those that a mesh axis runs over, the one named last changes fastest.
Arguments:
- panel: bfloat16 [8, 8, 1024, 1024], P('col', None, 'upd'), may hold values from -6 to 6
- diag_tiles: bfloat16 [8, 1024, 1024], P('col', 'upd'), may hold values from -6 to 6
- dinv: bfloat16 [8, 1024, 1024], P('col'), may hold values from -1 to 1, as said below
- u_fac: bfloat16 [8, 8, 4, 96, 1024], P('col', None, 'upd'), may hold values from -1.1953125 to 1.1953125
- v_fac: bfloat16 [8, 8, 4, 96, 1024], P('col', None, 'upd'), may hold values from -1.1953125 to 1.1953125
- ranks: int32 [8, 8, 4], P('col', None, 'upd'), may hold values from 1 to 96, as said below
- sketch: bfloat16 [8, 64, 1024], P('col'), may hold values from -6 to 6
Outputs:
- panel_out: bfloat16 [8, 8, 1024, 1024], P('col', None, 'upd')
- diag_out: float32 [8, 1024, 1024], P('col', 'upd')
Inputs may be any that keep to these rules, and one draw needn't show every extreme that they name: `ranks`: in every panel tile at least two of the 4 pieces have rank 96. `dinv`: each block is lower triangular with a positive diagonal.
All inputs are finite; a program needn't handle non-finite values.
Results may differ from a plain program's by a relative error of at most 0.014.
Values may be sent and summed in bfloat16 or wider, within the bound.
A program may use at most 64 MiB of HBM per device.

v0:
```python
import jax
import jax.numpy as jnp
from jax import lax
from jax.sharding import PartitionSpec as P


def shifted(block, axis, distance):
    devices = range(lax.axis_size(axis))
    route = [(i - distance, i) for i in devices if i - distance in devices]
    return lax.ppermute(block, axis, route)


def orthonormal(summed):
    gram = jnp.einsum("kb,lb->kl", summed, summed, precision=lax.Precision.HIGHEST)
    chol = jnp.linalg.cholesky(gram)
    return jax.scipy.linalg.solve_triangular(chol, summed, lower=True).astype(jnp.bfloat16)


def local(panel, diag_tiles, dinv, u_fac, v_fac, ranks, sketch):
    left_factor = u_fac[0, :, 0]
    right_factor = v_fac[0, :, 0]
    slots = lax.broadcasted_iota(jnp.int32, (1, left_factor.shape[1], 1), 1)
    keep = slots < ranks[0, :, 0][:, None, None]
    random_probe = jnp.einsum(
        "jef,yf->jey", right_factor, sketch[0], preferred_element_type=jnp.float32
    )
    random_probe = jnp.where(keep, random_probe, 0.0).astype(jnp.bfloat16)
    range_component = jnp.einsum(
        "zgj,zgp->zpj", left_factor, random_probe, preferred_element_type=jnp.float32
    )
    summed = lax.psum(range_component.astype(jnp.bfloat16), "upd").astype(jnp.float32)
    range_basis = jax.vmap(orthonormal)(summed)
    coefficient_matrix = jnp.einsum(
        "wxj,wuj->wxu", left_factor, range_basis, preferred_element_type=jnp.float32
    )
    coefficient_matrix = jnp.where(keep, coefficient_matrix, 0.0).astype(jnp.bfloat16)
    cross_term_part = jnp.einsum(
        "zgj,zgp->zpj", right_factor, coefficient_matrix, preferred_element_type=jnp.float32
    )
    cross_term = lax.psum(cross_term_part.astype(jnp.bfloat16), "upd")
    rows_dev = panel.shape[2]
    first_row = lax.axis_index("upd") * rows_dev
    range_basis_rows = lax.dynamic_slice_in_dim(range_basis, first_row, rows_dev, 2)
    approximation = jnp.einsum(
        "fei,fej->fij", range_basis_rows, cross_term, preferred_element_type=jnp.float32
    )
    updated_tile = (panel[0].astype(jnp.float32) - approximation).astype(jnp.bfloat16)
    lowrank_factor = jnp.einsum(
        "vxn,en->vxe", updated_tile, dinv[0], preferred_element_type=jnp.float32
    ).astype(jnp.bfloat16)
    band = lowrank_factor.shape[0]
    received = jnp.stack(
        [shifted(lowrank_factor[offset - 1], "col", offset) for offset in range(1, band + 1)]
    )
    columns = lax.all_to_all(received, "upd", split_axis=2, concat_axis=1, tiled=True)
    total = lax.psum_scatter(
        (-jnp.einsum("mrc,mnc->rn", columns, columns, preferred_element_type=jnp.float32)).astype(
            jnp.bfloat16
        ),
        "upd",
        scatter_dimension=0,
        tiled=True,
    ).astype(jnp.float32)
    diag_out = (diag_tiles[0].astype(jnp.float32) + total)[None]
    return (lowrank_factor[None], diag_out)


def solution(mesh):
    in_specs = (
        P("col", None, "upd", None),
        P("col", "upd", None),
        P("col", None, None),
        P("col", None, "upd", None, None),
        P("col", None, "upd", None, None),
        P("col", None, "upd"),
        P("col", None, None),
    )
    out_specs = (P("col", None, "upd", None), P("col", "upd", None))
    return jax.shard_map(local, mesh=mesh, in_specs=in_specs, out_specs=out_specs, check_vma=False)
```

profile of v0, /device:TPU:29, one launch (start us, length us, event | category | flops | bytes accessed | tf_op | source)
XLA Modules:
  0.0 415.8 jit_solution(16789103019356209810)
XLA Ops:
  8.1 3.9 fusion.22
  12.1 36.7 %all-reduce.3.cloned.1.call-done = bf16[8,64,1024]{2,1,0:T(8,128)(2,1)} async-done(((bf16[8,64,1024]{2,1,0:T(8,128)(2,1)}), bf16[8,64,1024]{2,1,0:T(8,128)(2,1)}) %all-reduce.3.cloned.1.call-update) | async-done | bytes 1048592 | tf_op jit(solution)/shard_map/psum | solution.py:31
  48.8 2.0 fusion.56
  51.7 1.7 fusion.43
  53.3 47.6 %custom-call.8 = f32[8,64,64]{2,1,0:T(8,128)S(1)} custom-call(f32[8,64,64]{2,1,0:T(8,128)} %fusion.43), custom_call_target="Cholesky" | custom-call | tf_op jit(solution)/shard_map/vmap(jit(cholesky))/cholesky | solution.py:15
  101.9 40.0 %custom-call.9 = f32[8,1,64,64]{2,3,1,0:T(8,128)S(1)} custom-call(f32[8,1,64,64]{3,2,1,0:T(8,128)} %select_bitcast_fusion), custom_call_target="InvertDiagBlocksLowerTriangular" | custom-call | tf_op jit(solution)/shard_map/vmap(jit(_solve_triangular))/triangular_solve | solution.py:16
  142.0 2.0 convolution_convert_fusion
  144.0 4.1 fusion.19
  148.2 36.6 %all-reduce.5.cloned.1.call-done = bf16[8,64,1024]{2,1,0:T(8,128)(2,1)} async-done(((bf16[8,64,1024]{2,1,0:T(8,128)(2,1)}), bf16[8,64,1024]{2,1,0:T(8,128)(2,1)}) %all-reduce.5.cloned.1.call-update) | async-done | bytes 1048592 | tf_op jit(solution)/shard_map/psum | solution.py:40
  184.8 9.0 %fusion.7 = bf16[8,256,1024]{2,1,0:T(8,128)(2,1)} fusion(bf16[1,8,256,1024]{3,2,1,0:T(8,128)(2,1)} %param.7, bf16[8,64,1024]{2,1,0:T(8,128)(2,1)} %all-reduce.5.cloned.1.call-done, bf16[1,1024,1024]{2,1,0:T(8,128)(2,1)S(1)} %copy-done, bf16[8,64,1024]{2,1,0:T(8,128)(2,1)} %convolution_convert_fusion, s32[]{:T(128)S(6)} %select_n.17), kind=kOutput, calls=%fused_computation.7 | convolution fusion | flops 4571791360 | bytes 11796484 | tf_op jit(solution)/shard_map/vxn,en->vxe/dot_general | solution.py:48
  193.8 2.6 slice_bitcast_fusion
  196.4 1.3 collective-permute-start
  197.7 1.3 collective-permute-start.1
  199.0 1.3 collective-permute-start.2
  201.0 1.3 collective-permute-start.6
  202.3 8.3 %collective-permute-done = bf16[256,1024]{1,0:T(8,128)(2,1)S(1)} collective-permute-done((bf16[256,1024]{1,0:T(8,128)(2,1)S(1)}, bf16[256,1024]{1,0:T(8,128)(2,1)S(1)}, u32[]{:S(2)}, u32[]{:S(2)}) %collective-permute-start) | collective-permute-done | bytes 524320 | tf_op jit(solution)/shard_map/ppermute | solution.py:10
  212.7 9.1 %collective-permute-done.1 = bf16[256,1024]{1,0:T(8,128)(2,1)S(1)} collective-permute-done((bf16[256,1024]{1,0:T(8,128)(2,1)S(1)}, bf16[256,1024]{1,0:T(8,128)(2,1)S(1)}, u32[]{:S(2)}, u32[]{:S(2)}) %collective-permute-start.1) | collective-permute-done | bytes 524320 | tf_op jit(solution)/shard_map/ppermute | solution.py:10
  226.8 62.4 %collective-permute-done.3 = bf16[256,1024]{1,0:T(8,128)(2,1)S(1)} collective-permute-done((bf16[256,1024]{1,0:T(8,128)(2,1)S(1)}, bf16[256,1024]{1,0:T(8,128)(2,1)S(1)}, u32[]{:S(2)}, u32[]{:S(2)}) %collective-permute-start.3) | collective-permute-done | bytes 524320 | tf_op jit(solution)/shard_map/ppermute | solution.py:10
  293.4 6.9 %copy.18 = bf16[8,256,1024]{1,0,2:T(8,128)(2,1)} copy(bf16[8,256,1024]{2,1,0:T(8,128)(2,1)} %bitcast_dynamic-update-slice_fusion) | data formatting | bytes 8388608 | tf_op jit(solution)/shard_map/stack | solution.py:52
  300.3 54.9 %all_to_all.18 = bf16[8,256,1024]{1,0,2:T(8,128)(2,1)} all-to-all(bf16[8,256,1024]{1,0,2:T(8,128)(2,1)} %copy.18), channel_id=1, replica_groups=mesh['upd'=4,'col'=8] {'upd'}, dimensions={2} | all-to-all | bytes 8388608 | tf_op jit(solution)/shard_map/all_to_all | solution.py:55
  355.2 7.5 %copy.19 = bf16[8,256,4,256]{3,1,2,0:T(8,128)(2,1)} copy(bf16[8,256,4,256]{1,0,3,2:T(8,128)(2,1)} %bitcast.106) | data formatting | bytes 8388608 | tf_op jit(solution)/shard_map/all_to_all | solution.py:55
  362.7 9.3 %fusion.4 = bf16[1024,1024]{1,0:T(8,128)(2,1)} fusion(bf16[8,1024,256]{2,1,0:T(8,128)(2,1)} %bitcast.108), kind=kOutput, calls=%fused_computation.5 | convolution fusion | flops 4297064448 | bytes 6291456 | tf_op jit(solution)/shard_map/mrc,mnc->rn/dot_general | solution.py:57
  372.1 35.0 %reduce-scatter.2.cloned.1.call-done = bf16[256,1024]{1,0:T(8,128)(2,1)} async-done(((bf16[1024,1024]{1,0:T(8,128)(2,1)}), bf16[256,1024]{1,0:T(8,128)(2,1)}) %reduce-scatter.2.cloned.1.call-update) | async-done | bytes 524304 | tf_op jit(solution)/shard_map/reduce_scatter | solution.py:56
  407.1 2.2 fusion.41
  (36 shorter events, 14.9 us)
Async XLA Ops:
  7.2 177.7 %copy-start = (bf16[1,1024,1024]{2,1,0:T(8,128)(2,1)S(1)}, bf16[1,1024,1024]{2,1,0:T(8,128)(2,1)}, u32[]{:S(2)}) copy-start(bf16[1,1024,1024]{2,1,0:T(8,128)(2,1)} %param.9) | copy-start | bytes 6291460
  7.2 41.6 %all-reduce.3.cloned.1.call-start = ((), (), s32[]{:S(2)}) async-start(), calls=%async_computation.2 | async-start | bytes 2097152 | tf_op jit(solution)/shard_map/psum | solution.py:31
  12.0 172.8 %all-reduce.5.cloned.1.call-start = ((), (), s32[]{:S(2)}) async-start(), calls=%async_computation.3 | async-start | bytes 2097152 | tf_op jit(solution)/shard_map/psum | solution.py:40
  48.8 93.2 %copy-start.1 = (bf16[8,64,1024]{2,1,0:T(8,128)(2,1)S(1)}, bf16[8,64,1024]{2,1,0:T(8,128)(2,1)}, u32[]{:S(2)}) copy-start(bf16[8,64,1024]{2,1,0:T(8,128)(2,1)} %all-reduce.3.cloned.1.call-done) | copy-start | bytes 3145732
  148.2 258.9 %reduce-scatter.2.cloned.1.call-start = ((), (), s32[]{:S(2)}) async-start(), calls=%async_computation.4 | async-start | bytes 2621440 | tf_op jit(solution)/shard_map/reduce_scatter | solution.py:56
  196.4 14.2 %collective-permute-start = (bf16[256,1024]{1,0:T(8,128)(2,1)S(1)}, bf16[256,1024]{1,0:T(8,128)(2,1)S(1)}, u32[]{:S(2)}, u32[]{:S(2)}) collective-permute-start(bf16[256,1024]{1,0:T(8,128)(2,1)S(1)} %get-tuple-element.9), channel_id=1, source_target_pairs={{0,1},{1,2},{2,3},{3,4},{4,5},{5,6},{6,7},{8,9},{9,10},{10,11},{11... | collective-permute-start | bytes 1572872 | tf_op jit(solution)/shard_map/ppermute | solution.py:10
  197.7 24.1 %collective-permute-start.1 = (bf16[256,1024]{1,0:T(8,128)(2,1)S(1)}, bf16[256,1024]{1,0:T(8,128)(2,1)S(1)}, u32[]{:S(2)}, u32[]{:S(2)}) collective-permute-start(bf16[256,1024]{1,0:T(8,128)(2,1)S(1)} %get-tuple-element.8), channel_id=1, source_target_pairs={{0,2},{1,3},{2,4},{3,5},{4,6},{5,7},{8,10},{9,11},{10,12},{11,13},... | collective-permute-start | bytes 1572872 | tf_op jit(solution)/shard_map/ppermute | solution.py:10
  199.0 25.7 %collective-permute-start.2 = (bf16[256,1024]{1,0:T(8,128)(2,1)S(1)}, bf16[256,1024]{1,0:T(8,128)(2,1)S(1)}, u32[]{:S(2)}, u32[]{:S(2)}) collective-permute-start(bf16[256,1024]{1,0:T(8,128)(2,1)S(1)} %get-tuple-element.7), channel_id=1, source_target_pairs={{0,3},{1,4},{2,5},{3,6},{4,7},{8,11},{9,12},{10,13},{11,14},{12,15... | collective-permute-start | bytes 1572872 | tf_op jit(solution)/shard_map/ppermute | solution.py:10
  200.3 92.2 %collective-permute-start.7 = (bf16[256,1024]{1,0:T(8,128)(2,1)S(1)}, bf16[256,1024]{1,0:T(8,128)(2,1)S(1)}, u32[]{:S(2)}, u32[]{:S(2)}) collective-permute-start(bf16[256,1024]{1,0:T(8,128)(2,1)S(1)} %get-tuple-element.2), channel_id=1, source_target_pairs={} | collective-permute-start | bytes 1572872 | tf_op jit(solution)/shard_map/ppermute | solution.py:10
  201.0 90.7 %collective-permute-start.6 = (bf16[256,1024]{1,0:T(8,128)(2,1)S(1)}, bf16[256,1024]{1,0:T(8,128)(2,1)S(1)}, u32[]{:S(2)}, u32[]{:S(2)}) collective-permute-start(bf16[256,1024]{1,0:T(8,128)(2,1)S(1)} %get-tuple-element.3), channel_id=1, source_target_pairs={{0,7},{8,15},{16,23},{24,31}} | collective-permute-start | bytes 1572872 | tf_op jit(solution)/shard_map/ppermute | solution.py:10
  210.6 78.6 %collective-permute-start.3 = (bf16[256,1024]{1,0:T(8,128)(2,1)S(1)}, bf16[256,1024]{1,0:T(8,128)(2,1)S(1)}, u32[]{:S(2)}, u32[]{:S(2)}) collective-permute-start(bf16[256,1024]{1,0:T(8,128)(2,1)S(1)} %get-tuple-element.6), channel_id=1, source_target_pairs={{0,4},{1,5},{2,6},{3,7},{8,12},{9,13},{10,14},{11,15},{16,20},{17,... | collective-permute-start | bytes 1572872 | tf_op jit(solution)/shard_map/ppermute | solution.py:10
  221.8 68.2 %collective-permute-start.4 = (bf16[256,1024]{1,0:T(8,128)(2,1)S(1)}, bf16[256,1024]{1,0:T(8,128)(2,1)S(1)}, u32[]{:S(2)}, u32[]{:S(2)}) collective-permute-start(bf16[256,1024]{1,0:T(8,128)(2,1)S(1)} %get-tuple-element.5), channel_id=1, source_target_pairs={{0,5},{1,6},{2,7},{8,13},{9,14},{10,15},{16,21},{17,22},{18,23},{2... | collective-permute-start | bytes 1572872 | tf_op jit(solution)/shard_map/ppermute | solution.py:10
  224.6 66.2 %collective-permute-start.5 = (bf16[256,1024]{1,0:T(8,128)(2,1)S(1)}, bf16[256,1024]{1,0:T(8,128)(2,1)S(1)}, u32[]{:S(2)}, u32[]{:S(2)}) collective-permute-start(bf16[256,1024]{1,0:T(8,128)(2,1)S(1)} %get-tuple-element.4), channel_id=1, source_target_pairs={{0,6},{1,7},{8,14},{9,15},{16,22},{17,23},{24,30},{25,31}} | collective-permute-start | bytes 1572872 | tf_op jit(solution)/shard_map/ppermute | solution.py:10
  362.7 44.4 %copy-start.2 = (bf16[1,256,1024]{2,1,0:T(8,128)(2,1)S(1)}, bf16[1,256,1024]{2,1,0:T(8,128)(2,1)}, u32[]{:S(2)}) copy-start(bf16[1,256,1024]{2,1,0:T(8,128)(2,1)} %param.8) | copy-start | bytes 1572868
Sparse Core Ops, SparseCore 0:
  12.1 36.5 all-reduce.2
  148.3 36.4 all-reduce.4
  372.2 34.8 reduce-scatter.1
where the time goes:
time: 418 us; the launch traced here: 416 us
  waiting for transfers between devices  189 us (45%)
  other arithmetic  93.4 us (22%)
  blocking collectives  54.9 us (13%)
  matrix products  30.4 us (7%)
  local copies, waits for them, and re-layouts  24.6 us (6%)
  between operations  13.9 us (3%)
  starting transfers between devices  9.82 us (2%)
    ppermute x8, waiting for transfers between devices, shifted(): return lax.ppermute(block, axis, route)  80.5 us
    all_to_all x1, blocking collectives, local(): lax.all_to_all(received, 'upd', split_axis=2, concat_axis=1, tiled=True)  54.9 us
    another operation x4, other arithmetic, orthonormal(): chol = jnp.linalg.cholesky(gram)  47.8 us
    another operation x3, other arithmetic, orthonormal(): jax.scipy.linalg.solve_triangular(chol, summed, lower=True)  40.9 us
    psum x1, waiting for transfers between devices, local(): lax.psum(range_component.astype(jnp.bfloat16), 'upd').astype(jnp.float32)  36.7 us
    psum x1, waiting for transfers between devices, local(): cross_term = lax.psum(cross_term_part.astype(jnp.bfloat16), 'upd')  36.6 us
    reduce_scatter x1, waiting for transfers between devices, local(): lax.psum_scatter((-jnp.einsum('mrc,mnc->rn', columns, columns, preferred_...  35 us
    ppermute x8, starting transfers between devices, shifted(): return lax.ppermute(block, axis, route)  9.7 us
  transfers between devices with their start and end apart: 11, of which 7 were waited for; matrix products, arithmetic and copies ran while one was open for 1% of the time, Pallas kernels for 0%

commit v1 on v0

v1 whole, which is shorter than its diff:
```python
import functools

import jax
import jax.numpy as jnp
from jax import lax
from jax.experimental import pallas as pl
from jax.experimental.pallas import tpu as pltpu
from jax.sharding import PartitionSpec as P

F32 = jnp.float32
BF16 = jnp.bfloat16
NT = (((1,), (1,)), ((), ()))
TN = (((0,), (0,)), ((), ()))
NN = (((1,), (0,)), ((), ()))


def dot(a, b, dims):
    return lax.dot_general(a, b, dims, preferred_element_type=F32)


def dot_high(a, b, dims):
    return lax.dot_general(
        a, b, dims, precision=lax.Precision.HIGHEST, preferred_element_type=F32
    )


def inverse_factor(aug):
    size = aug.shape[1]
    rows = lax.broadcasted_iota(jnp.int32, (1, size, 1), 1)
    for j in range(size - 1):
        pivot = aug[:, j : j + 1, :]
        scaled = pivot / aug[:, j : j + 1, j : j + 1]
        column = jnp.where(rows > j, aug[:, :, j : j + 1], 0.0)
        aug = aug - column * scaled
    at_row = lax.broadcasted_iota(jnp.int32, (1, size, 2 * size), 1)
    at_col = lax.broadcasted_iota(jnp.int32, (1, size, 2 * size), 2)
    diagonal = jnp.sum(jnp.where(at_row == at_col, aug, 0.0), axis=2, keepdims=True)
    return jnp.where(at_col >= size, aug / jnp.sqrt(diagonal), 0.0)


def kernel(
    U, C,
    panel, diag, dinv, uf, vf, keep, sketch,
    out, diag_out,
    t0f, t0b, rx, bx, ex, r, r_rx, basis, xp, x_rx, e, tc, part, p_rx,
    t_s, t_r, bx_s, bx_r, ex_s, ex_r, r_s, r_r, b_s, b_r, x_s, x_r, e_s, e_r, p_s, p_r,
):
    M, RD, B = panel.shape[1:]
    K = sketch.shape[1]
    CB = B // U
    MT = M // U
    me_u, me_c = lax.axis_index("upd"), lax.axis_index("col")

    def copy(src, dst, send, recv, u, c):
        return pltpu.make_async_remote_copy(
            src_ref=src, dst_ref=dst, send_sem=send, recv_sem=recv,
            device_id={"upd": u, "col": c}, device_id_type=pl.DeviceIdType.MESH,
        )

    def after(k):
        return lax.rem(me_u + k, U)

    def before(k):
        return lax.rem(me_u + U - k, U)

    own = pl.ds(me_u * MT, MT)

    def tiles(u):
        return pl.ds(u * MT, MT)

    def to_column(m):
        return me_c + m + 1

    barrier = pltpu.get_barrier_semaphore()

    def greet(u, c):
        pl.semaphore_signal(
            barrier, inc=1, device_id={"upd": u, "col": c}, device_id_type=pl.DeviceIdType.MESH
        )

    for k in range(1, U):
        greet(after(k), me_c)

    @pl.loop(0, M)
    def _(m):
        @pl.when(me_c + m + 1 < C)
        def _():
            for v in range(U):
                greet(v, me_c + m + 1)

        @pl.when(me_c - m - 1 >= 0)
        def _():
            for v in range(U):
                greet(v, me_c - m - 1)

    @pl.loop(0, M)
    def _(t):
        probe = (dot(sketch[0], vf[0, t, 0], NT) * keep[t]).astype(BF16)
        r[t] = dot(probe, uf[0, t, 0], NN).astype(BF16)

    pl.semaphore_wait(
        barrier, U - 1 + U * (jnp.minimum(M, C - 1 - me_c) + jnp.minimum(M, me_c))
    )

    def scatter_out(buf, k, land, send, recv):
        return copy(
            buf.at[tiles(after(k))], land.at[k - 1], send.at[k - 1], recv.at[k - 1], after(k), me_c
        )

    for k in range(1, U):
        scatter_out(r, k, r_rx, r_s, r_r).start()

    def t_copy(m, v):
        return copy(
            t0b.at[m, v], rx.at[m, pl.ds(me_u * RD, RD)],
            t_s.at[m, v], t_r.at[m, me_u], v, to_column(m),
        )

    @pl.loop(0, M)
    def _(m):
        for v in range(U):
            block = dot(panel[0, m], dinv[0, v * CB : (v + 1) * CB, :], NT)
            t0f[m, :, v * CB : (v + 1) * CB] = block
            t0b[m, v] = block.astype(BF16)

        @pl.when(to_column(m) < C)
        def _():
            for v in range(U):
                t_copy(m, v).start()

    for k in range(1, U):
        scatter_out(r, k, r_rx, r_s, r_r).wait_recv()

    summed = r[own].astype(F32)
    for k in range(1, U):
        summed = summed + r_rx[k - 1].astype(F32)
    zeros = jnp.zeros((K, B), F32)
    at_row = lax.broadcasted_iota(jnp.int32, (K, 2 * K), 0)
    at_col = lax.broadcasted_iota(jnp.int32, (K, 2 * K), 1)
    eye = jnp.where(at_col == at_row + K, 1.0, 0.0).astype(F32)
    grams = [
        dot_high(summed[i], jnp.concatenate([summed[i], zeros], axis=0), NT) + eye
        for i in range(MT)
    ]
    inverse = inverse_factor(jnp.stack(grams))
    for i in range(MT):
        basis[me_u * MT + i] = dot_high(
            inverse[i], jnp.concatenate([zeros, summed[i]], axis=0), NN
        ).astype(BF16)

    def gather_out(buf, k, send, recv):
        return copy(buf.at[own], buf.at[own], send.at[k - 1], recv.at[k - 1], after(k), me_c)

    def gather_in(buf, k, send, recv):
        region = buf.at[tiles(before(k))]
        return copy(region, region, send.at[k - 1], recv.at[k - 1], after(k), me_c)

    for k in range(1, U):
        gather_out(basis, k, b_s, b_r).start()
    for k in range(1, U):
        gather_in(basis, k, b_s, b_r).wait_recv()

    def project(t):
        coeff = (dot(basis[t], uf[0, t, 0], NT) * keep[t]).astype(BF16)
        xp[t] = dot(coeff, vf[0, t, 0], NN).astype(BF16)

    @pl.loop(0, M)
    def _(t):
        project(t)

    for k in range(1, U):
        scatter_out(xp, k, x_rx, x_s, x_r).start()

    def b_copy(m):
        return copy(basis.at[m], bx.at[m], bx_s.at[m], bx_r.at[m], me_u, to_column(m))

    @pl.loop(0, M)
    def _(m):
        @pl.when(to_column(m) < C)
        def _():
            b_copy(m).start()

    for k in range(1, U):
        scatter_out(xp, k, x_rx, x_s, x_r).wait_recv()

    cross = xp[own].astype(F32)
    for k in range(1, U):
        cross = cross + x_rx[k - 1].astype(F32)
    cross = cross.astype(BF16)
    for i in range(MT):
        for v in range(U):
            e[me_u * MT + i, v] = dot(
                cross[i], dinv[0, v * CB : (v + 1) * CB, :], NT
            ).astype(BF16)

    def e_copy(i, v):
        m = me_u * MT + i
        return copy(e.at[m, v], ex.at[m], ex_s.at[i, v], ex_r.at[m], v, to_column(m))

    for i in range(MT):
        @pl.when(to_column(me_u * MT + i) < C)
        def _():
            for v in range(U):
                e_copy(i, v).start()

    for k in range(1, U):
        gather_out(e, k, e_s, e_r).start()
    for k in range(1, U):
        gather_in(e, k, e_s, e_r).wait_recv()

    @pl.loop(0, M)
    def _(m):
        rows = basis[m, :, pl.ds(pl.multiple_of(me_u * RD, RD), RD)]
        for v in range(U):
            cols = slice(v * CB, (v + 1) * CB)
            out[0, m, :, cols] = (t0f[m, :, cols] - dot(rows, e[m, v], TN)).astype(BF16)

    for m in range(M):
        cols = slice(m * CB, (m + 1) * CB)

        @pl.when(me_c - m - 1 >= 0)
        def _():
            @pl.loop(0, U)
            def _(s):
                copy(
                    t0b.at[m, 0], rx.at[m, pl.ds(s * RD, RD)],
                    t_s.at[m, 0], t_r.at[m, s], me_u, me_c,
                ).wait_recv()

            b_copy(m).wait_recv()
            copy(e.at[m, 0], ex.at[m], ex_s.at[0, 0], ex_r.at[m], me_u, me_c).wait_recv()

            @pl.loop(0, U)
            def _(s):
                rows = pl.ds(pl.multiple_of(s * RD, RD), RD)
                change = dot(bx[m, :, rows], ex[m], TN)
                tc[rows, cols] = (rx[m, rows, :].astype(F32) - change).astype(BF16)

        @pl.when(me_c - m - 1 < 0)
        def _():
            tc[:, cols] = jnp.zeros((B, CB), BF16)

    def p_copy(k):
        return copy(
            part.at[k - 1], p_rx.at[k - 1], p_s.at[k - 1], p_r.at[k - 1], after(k), me_c
        )

    def product(u):
        return dot(tc[pl.ds(pl.multiple_of(u * RD, RD), RD), :], tc[...], NT)

    @pl.loop(1, U)
    def _(k):
        part[k - 1] = product(after(k)).astype(BF16)
        p_copy(k).start()

    diag_out[0] = diag[0].astype(F32) - product(me_u)
    for k in range(1, U):
        p_copy(k).wait_recv()
        diag_out[0] = diag_out[0] - p_rx[k - 1].astype(F32)

    for k in range(1, U):
        scatter_out(r, k, r_rx, r_s, r_r).wait_send()
        gather_out(basis, k, b_s, b_r).wait_send()
        scatter_out(xp, k, x_rx, x_s, x_r).wait_send()
        gather_out(e, k, e_s, e_r).wait_send()
        p_copy(k).wait_send()
    for i in range(MT):
        @pl.when(to_column(me_u * MT + i) < C)
        def _():
            for v in range(U):
                e_copy(i, v).wait_send()

    @pl.loop(0, M)
    def _(m):
        @pl.when(to_column(m) < C)
        def _():
            for v in range(U):
                t_copy(m, v).wait_send()
            b_copy(m).wait_send()


def local(U, C, panel, diag_tiles, dinv, u_fac, v_fac, ranks, sketch):
    M, RD, B = panel.shape[1:]
    R = u_fac.shape[3]
    K = sketch.shape[1]
    CB, MT = B // U, M // U
    slots = lax.broadcasted_iota(jnp.int32, (M, 1, R), 2)
    keep = (slots < ranks[0, :, 0][:, None, None]).astype(F32)
    dma = pltpu.SemaphoreType.DMA
    peers = [dma((U - 1,))] * 2
    vmem = pl.BlockSpec(memory_space=pltpu.VMEM)
    return pl.pallas_call(
        functools.partial(kernel, U, C),
        out_shape=(
            jax.ShapeDtypeStruct(panel.shape, BF16),
            jax.ShapeDtypeStruct(diag_tiles.shape, F32),
        ),
        in_specs=[vmem] * 7,
        out_specs=(vmem, vmem),
        scratch_shapes=[
            pltpu.VMEM((M, RD, B), F32),
            pltpu.VMEM((M, U, RD, CB), BF16),
            pltpu.VMEM((M, B, CB), BF16),
            pltpu.VMEM((M, K, B), BF16),
            pltpu.VMEM((M, K, CB), BF16),
            pltpu.VMEM((M, K, B), BF16),
            pltpu.VMEM((U - 1, MT, K, B), BF16),
            pltpu.VMEM((M, K, B), BF16),
            pltpu.VMEM((M, K, B), BF16),
            pltpu.VMEM((U - 1, MT, K, B), BF16),
            pltpu.VMEM((M, U, K, CB), BF16),
            pltpu.VMEM((B, M * CB), BF16),
            pltpu.VMEM((U - 1, RD, B), BF16),
            pltpu.VMEM((U - 1, RD, B), BF16),
            dma((M, U)), dma((M, U)), dma((M,)), dma((M,)), dma((MT, U)), dma((M,)),
            *peers, *peers, *peers, *peers, *peers,
        ],
        compiler_params=pltpu.CompilerParams(
            collective_id=0, has_side_effects=True, vmem_limit_bytes=58 * 1024 * 1024
        ),
        name="band_window",
    )(panel, diag_tiles, dinv, u_fac, v_fac, keep, sketch)


def solution(mesh):
    in_specs = (
        P("col", None, "upd", None),
        P("col", "upd", None),
        P("col", None, None),
        P("col", None, "upd", None, None),
        P("col", None, "upd", None, None),
        P("col", None, "upd"),
        P("col", None, None),
    )
    out_specs = (P("col", None, "upd", None), P("col", "upd", None))
    body = functools.partial(local, mesh.shape["upd"], mesh.shape["col"])
    return jax.shard_map(body, mesh=mesh, in_specs=in_specs, out_specs=out_specs, check_vma=False)
```

time: 418 us -> 182 us (0.44)
  waiting for transfers between devices: 189 us -> 0 us
  Pallas kernels: 0 us -> 174 us
  other arithmetic: 93.4 us -> 1.32 us
  blocking collectives: 54.9 us -> 0 us
  matrix products: 30.4 us -> 0 us
  local copies, waits for them, and re-layouts: 24.6 us -> 5.7 us
  between operations: 13.9 us -> 0.65 us
  starting transfers between devices: 9.82 us -> 0 us
    pallas_call x0 -> x1, Pallas kernels: none -> 174 us  [local(): pl.pallas_call(functools.partial(kernel, U, C), out_shape=(jax.ShapeDtype...]
    another operation x7 -> x0, other arithmetic: 88.6 us -> none  [the longest x4 47.8 us: orthonormal(): chol = jnp.linalg.cholesky(gram)]
    ppermute x8 -> x0, waiting for transfers between devices: 80.5 us -> none  [shifted(): return lax.ppermute(block, axis, route)]
    psum x2 -> x0, waiting for transfers between devices: 73.2 us -> none  [the longest x1 36.7 us: local(): lax.psum(range_component.astype(jnp.bfloat16), 'upd').astype(jnp.float32)]
    all_to_all x1 -> x0, blocking collectives: 54.9 us -> none  [local(): lax.all_to_all(received, 'upd', split_axis=2, concat_axis=1, tiled=True)]
    reduce_scatter x1 -> x0, waiting for transfers between devices: 35 us -> none  [local(): lax.psum_scatter((-jnp.einsum('mrc,mnc->rn', columns, columns, preferred_...]
    dot_general x5 -> x0, matrix products: 28.4 us -> none  [the longest x1 9.34 us: local(): jnp.einsum('mrc,mnc->rn', columns, columns, preferred_element_type=jnp.fl...]
    ppermute x8 -> x0, starting transfers between devices: 9.7 us -> none  [shifted(): return lax.ppermute(block, axis, route)]
  transfers between devices with their start and end apart: 11 -> 0, of which waited for: 7 -> 0; matrix products, arithmetic and copies ran while one was open for 1% -> 0% of each run, Pallas kernels for 0% -> 0%
where the time goes in v1:
time: 182 us; the launch traced here: 181 us
  Pallas kernels  174 us (96%)
  local copies, waits for them, and re-layouts  5.7 us (3%)
    pallas_call x1, Pallas kernels, local(): pl.pallas_call(functools.partial(kernel, U, C), out_shape=(jax.ShapeDtype...  174 us
    unnamed x4, local copies, waits for them, and re-layouts  5.7 us

profile of v1, /device:TPU:29, one launch (start us, length us, event | category | flops | bytes accessed | tf_op | source)
XLA Modules:
  0.0 181.4 jit_solution(18290269423259684972)
XLA Ops:
  0.6 1.3 compare_convert_fusion.keep
  2.0 173.7 %band_window.1 = (bf16[1,8,256,1024]{3,2,1,0:T(8,128)(2,1)}, f32[1,256,1024]{2,1,0:T(8,128)}) custom-call(bf16[1,8,256,1024]{3,2,1,0:T(8,128)(2,1)} %panel.1, bf16[1,256,1024]{2,1,0:T(8,128)(2,1)} %diag.1, bf16[1,1024,1024]{2,1,0:T(8,128)(2,1)} %dinv.1, bf16[1,8,1,96,1024]{4,3,2,1,0:T(8,128)(2,1)} %uf.1, bf16[1,8,1,96,1024]{4,3,2,1,0:T(8,128)(2,1)} %vf.1, ...), custom_call_target="tpu_custom_call" | custom-call | tf_op jit(solution)/shard_map/band_window/pallas_call | solution.py:292
  175.6 0.0 copy-start
  175.6 4.7 %copy.11 = bf16[1,8,256,1024]{3,2,1,0:T(8,128)(2,1)} copy(bf16[1,8,256,1024]{3,2,1,0:T(8,128)(2,1)} %get-tuple-element.4) | data formatting | bytes 8388608
  180.4 0.0 copy-done
  180.4 1.0 copy.12
Async XLA Ops:
  175.6 4.7 %copy-start = (f32[1,256,1024]{2,1,0:T(8,128)S(1)}, f32[1,256,1024]{2,1,0:T(8,128)}, u32[]{:S(2)}) copy-start(f32[1,256,1024]{2,1,0:T(8,128)} %get-tuple-element.5) | copy-start | bytes 3145732

commit v2 on v1

--- a/solution.py
+++ b/solution.py
@@ -42,8 +42,9 @@
     U, C,
     panel, diag, dinv, uf, vf, keep, sketch,
     out, diag_out,
-    t0f, t0b, rx, bx, ex, r, r_rx, basis, xp, x_rx, e, tc, part, p_rx,
-    t_s, t_r, bx_s, bx_r, ex_s, ex_r, r_s, r_r, b_s, b_r, x_s, x_r, e_s, e_r, p_s, p_r,
+    t0f, t0b, tc, bf, f, r, r_rx, basis, xp, x_rx, e, acc, near, near_rx, far, far_rx,
+    t_s, t_r, bx_s, bx_r, f_s, f_r, r_s, r_r, b_s, b_r, x_s, x_r, e_s, e_r,
+    near_s, near_r, far_s, far_r,
 ):
     M, RD, B = panel.shape[1:]
     K = sketch.shape[1]
@@ -112,7 +113,8 @@
 
     def t_copy(m, v):
         return copy(
-            t0b.at[m, v], rx.at[m, pl.ds(me_u * RD, RD)],
+            t0b.at[m, v],
+            tc.at[pl.ds(me_u * RD, RD), pl.ds(pl.multiple_of(m * CB, CB), CB)],
             t_s.at[m, v], t_r.at[m, me_u], v, to_column(m),
         )
 
@@ -157,6 +159,16 @@
 
     for k in range(1, U):
         gather_out(basis, k, b_s, b_r).start()
+
+    def b_copy(i):
+        m = me_u * MT + i
+        return copy(basis.at[m], bf.at[i, 0], bx_s.at[i], bx_r.at[i], me_u, to_column(m))
+
+    for i in range(MT):
+        @pl.when(to_column(me_u * MT + i) < C)
+        def _():
+            b_copy(i).start()
+
     for k in range(1, U):
         gather_in(basis, k, b_s, b_r).wait_recv()
 
@@ -170,15 +182,6 @@
 
     for k in range(1, U):
         scatter_out(xp, k, x_rx, x_s, x_r).start()
-
-    def b_copy(m):
-        return copy(basis.at[m], bx.at[m], bx_s.at[m], bx_r.at[m], me_u, to_column(m))
-
-    @pl.loop(0, M)
-    def _(m):
-        @pl.when(to_column(m) < C)
-        def _():
-            b_copy(m).start()
 
     for k in range(1, U):
         scatter_out(xp, k, x_rx, x_s, x_r).wait_recv()
@@ -193,20 +196,28 @@
                 cross[i], dinv[0, v * CB : (v + 1) * CB, :], NT
             ).astype(BF16)
 
-    def e_copy(i, v):
-        m = me_u * MT + i
-        return copy(e.at[m, v], ex.at[m], ex_s.at[i, v], ex_r.at[m], v, to_column(m))
-
-    for i in range(MT):
-        @pl.when(to_column(me_u * MT + i) < C)
-        def _():
-            for v in range(U):
-                e_copy(i, v).start()
-
     for k in range(1, U):
         gather_out(e, k, e_s, e_r).start()
     for k in range(1, U):
         gather_in(e, k, e_s, e_r).wait_recv()
+
+    def f_copy(m, i):
+        return copy(
+            f.at[m], bf.at[i, 1, :, pl.ds(pl.multiple_of(me_u * RD, RD), RD)],
+            f_s.at[m], f_r.at[i, me_u], m // MT, to_column(m),
+        )
+
+    for m in range(M):
+        @pl.when(to_column(m) < C)
+        def _():
+            rows = basis[m, :, pl.ds(pl.multiple_of(me_u * RD, RD), RD)]
+            left = jnp.zeros((K, RD), F32)
+            square = jnp.zeros((K, K), F32)
+            for v in range(U):
+                left = left + dot(e[m, v], t0b[m, v], NT)
+                square = square + dot(e[m, v], e[m, v], NT)
+            f[m] = (left - 0.5 * dot_high(square, rows.astype(F32), NN)).astype(BF16)
+            f_copy(m, m % MT).start()
 
     @pl.loop(0, M)
     def _(m):
@@ -223,52 +234,88 @@
             @pl.loop(0, U)
             def _(s):
                 copy(
-                    t0b.at[m, 0], rx.at[m, pl.ds(s * RD, RD)],
+                    t0b.at[m, 0], tc.at[pl.ds(s * RD, RD), cols],
                     t_s.at[m, 0], t_r.at[m, s], me_u, me_c,
                 ).wait_recv()
 
-            b_copy(m).wait_recv()
-            copy(e.at[m, 0], ex.at[m], ex_s.at[0, 0], ex_r.at[m], me_u, me_c).wait_recv()
+        @pl.when(me_c - m - 1 < 0)
+        def _():
+            tc[:, cols] = jnp.zeros((B, CB), BF16)
+
+    def rows_of(u):
+        return pl.ds(pl.multiple_of(u * RD, RD), RD)
+
+    @pl.loop(0, U)
+    def _(u):
+        acc[rows_of(u), :] = dot(tc[rows_of(u), :], tc[...], NT)
+
+    for i in range(MT):
+        @pl.when(me_c - (me_u * MT + i) - 1 >= 0)
+        def _():
+            b_copy(i).wait_recv()
 
             @pl.loop(0, U)
             def _(s):
-                rows = pl.ds(pl.multiple_of(s * RD, RD), RD)
-                change = dot(bx[m, :, rows], ex[m], TN)
-                tc[rows, cols] = (rx[m, rows, :].astype(F32) - change).astype(BF16)
-
-        @pl.when(me_c - m - 1 < 0)
-        def _():
-            tc[:, cols] = jnp.zeros((B, CB), BF16)
-
-    def p_copy(k):
+                copy(
+                    f.at[0], bf.at[i, 1, :, pl.ds(pl.multiple_of(s * RD, RD), RD)],
+                    f_s.at[0], f_r.at[i, s], me_u, me_c,
+                ).wait_recv()
+
+        @pl.when(me_c - (me_u * MT + i) - 1 < 0)
+        def _():
+            bf[i] = jnp.zeros((2, K, B), BF16)
+
+    def product(u):
+        total = acc[rows_of(u), :]
+        for i in range(MT):
+            total = total - dot(bf[i, 0, :, rows_of(u)], bf[i, 1], TN)
+            total = total - dot(bf[i, 1, :, rows_of(u)], bf[i, 0], TN)
+        return total
+
+    X = U // 2
+    side = lax.rem(me_u, 2)
+    partner = me_u + 1 - 2 * side
+
+    def ahead(k):
+        return lax.rem(me_u + 2 * k, U)
+
+    def near_copy(k):
+        return copy(near.at[k], near_rx.at[k], near_s.at[k], near_r.at[k], partner, me_c)
+
+    def far_copy(k):
         return copy(
-            part.at[k - 1], p_rx.at[k - 1], p_s.at[k - 1], p_r.at[k - 1], after(k), me_c
-        )
-
-    def product(u):
-        return dot(tc[pl.ds(pl.multiple_of(u * RD, RD), RD), :], tc[...], NT)
-
-    @pl.loop(1, U)
-    def _(k):
-        part[k - 1] = product(after(k)).astype(BF16)
-        p_copy(k).start()
-
-    diag_out[0] = diag[0].astype(F32) - product(me_u)
-    for k in range(1, U):
-        p_copy(k).wait_recv()
-        diag_out[0] = diag_out[0] - p_rx[k - 1].astype(F32)
+            far.at[k - 1], far_rx.at[k - 1], far_s.at[k - 1], far_r.at[k - 1], ahead(k), me_c
+        )
+
+    for n in range(1, X + 1):
+        k = n % X
+        near[k] = product(ahead(k) + 1 - 2 * side).astype(BF16)
+        near_copy(k).start()
+    for k in range(1, X):
+        part = product(ahead(k))
+        near_copy(k).wait_recv()
+        far[k - 1] = (part + near_rx[k].astype(F32)).astype(BF16)
+        far_copy(k).start()
+    part = diag[0].astype(F32) - product(me_u)
+    near_copy(0).wait_recv()
+    diag_out[0] = part - near_rx[0].astype(F32)
+    for k in range(1, X):
+        far_copy(k).wait_recv()
+        diag_out[0] = diag_out[0] - far_rx[k - 1].astype(F32)
 
     for k in range(1, U):
         scatter_out(r, k, r_rx, r_s, r_r).wait_send()
         gather_out(basis, k, b_s, b_r).wait_send()
         scatter_out(xp, k, x_rx, x_s, x_r).wait_send()
         gather_out(e, k, e_s, e_r).wait_send()
-        p_copy(k).wait_send()
+    for k in range(X):
+        near_copy(k).wait_send()
+    for k in range(1, X):
+        far_copy(k).wait_send()
     for i in range(MT):
         @pl.when(to_column(me_u * MT + i) < C)
         def _():
-            for v in range(U):
-                e_copy(i, v).wait_send()
+            b_copy(i).wait_send()
 
     @pl.loop(0, M)
     def _(m):
@@ -276,14 +323,14 @@
         def _():
             for v in range(U):
                 t_copy(m, v).wait_send()
-            b_copy(m).wait_send()
+            f_copy(m, lax.rem(m, MT)).wait_send()
 
 
 def local(U, C, panel, diag_tiles, dinv, u_fac, v_fac, ranks, sketch):
     M, RD, B = panel.shape[1:]
     R = u_fac.shape[3]
     K = sketch.shape[1]
-    CB, MT = B // U, M // U
+    CB, MT, X = B // U, M // U, U // 2
     slots = lax.broadcasted_iota(jnp.int32, (M, 1, R), 2)
     keep = (slots < ranks[0, :, 0][:, None, None]).astype(F32)
     dma = pltpu.SemaphoreType.DMA
@@ -300,20 +347,23 @@
         scratch_shapes=[
             pltpu.VMEM((M, RD, B), F32),
             pltpu.VMEM((M, U, RD, CB), BF16),
-            pltpu.VMEM((M, B, CB), BF16),
-            pltpu.VMEM((M, K, B), BF16),
-            pltpu.VMEM((M, K, CB), BF16),
+            pltpu.VMEM((B, M * CB), BF16),
+            pltpu.VMEM((MT, 2, K, B), BF16),
+            pltpu.VMEM((M, K, RD), BF16),
             pltpu.VMEM((M, K, B), BF16),
             pltpu.VMEM((U - 1, MT, K, B), BF16),
             pltpu.VMEM((M, K, B), BF16),
             pltpu.VMEM((M, K, B), BF16),
             pltpu.VMEM((U - 1, MT, K, B), BF16),
             pltpu.VMEM((M, U, K, CB), BF16),
-            pltpu.VMEM((B, M * CB), BF16),
-            pltpu.VMEM((U - 1, RD, B), BF16),
-            pltpu.VMEM((U - 1, RD, B), BF16),
-            dma((M, U)), dma((M, U)), dma((M,)), dma((M,)), dma((MT, U)), dma((M,)),
-            *peers, *peers, *peers, *peers, *peers,
+            pltpu.VMEM((B, B), F32),
+            pltpu.VMEM((X, RD, B), BF16),
+            pltpu.VMEM((X, RD, B), BF16),
+            pltpu.VMEM((X - 1, RD, B), BF16),
+            pltpu.VMEM((X - 1, RD, B), BF16),
+            dma((M, U)), dma((M, U)), dma((MT,)), dma((MT,)), dma((M,)), dma((MT, U)),
+            *peers, *peers, *peers, *peers,
+            dma((X,)), dma((X,)), dma((X - 1,)), dma((X - 1,)),
         ],
         compiler_params=pltpu.CompilerParams(
             collective_id=0, has_side_effects=True, vmem_limit_bytes=58 * 1024 * 1024

time: 182 us -> 156 us (0.86)
  Pallas kernels: 174 us -> 148 us
    pallas_call x1, Pallas kernels: 174 us -> 148 us  [local(): pl.pallas_call(functools.partial(kernel, U, C), out_shape=(jax.ShapeDtype...]
where the time goes in v2:
time: 156 us
  Pallas kernels  148 us (95%)
  local copies, waits for them, and re-layouts  5.7 us (4%)
    pallas_call x1, Pallas kernels, local(): pl.pallas_call(functools.partial(kernel, U, C), out_shape=(jax.ShapeDtype...  148 us
    unnamed x4, local copies, waits for them, and re-layouts  5.7 us

profile of v2, /device:TPU:29, one launch (start us, length us, event | category | flops | bytes accessed | tf_op | source)
XLA Modules:
  0.0 156.0 jit_solution(12666433175148925228)
XLA Ops:
  0.6 1.3 compare_convert_fusion.keep
  2.0 148.3 %band_window.1 = (bf16[1,8,256,1024]{3,2,1,0:T(8,128)(2,1)}, f32[1,256,1024]{2,1,0:T(8,128)}) custom-call(bf16[1,8,256,1024]{3,2,1,0:T(8,128)(2,1)} %panel.1, bf16[1,256,1024]{2,1,0:T(8,128)(2,1)} %diag.1, bf16[1,1024,1024]{2,1,0:T(8,128)(2,1)} %dinv.1, bf16[1,8,1,96,1024]{4,3,2,1,0:T(8,128)(2,1)} %uf.1, bf16[1,8,1,96,1024]{4,3,2,1,0:T(8,128)(2,1)} %vf.1, ...), custom_call_target="tpu_custom_call" | custom-call | tf_op jit(solution)/shard_map/band_window/pallas_call | solution.py:339
  150.3 0.0 copy-start
  150.3 4.7 %copy.11 = bf16[1,8,256,1024]{3,2,1,0:T(8,128)(2,1)} copy(bf16[1,8,256,1024]{3,2,1,0:T(8,128)(2,1)} %get-tuple-element.4) | data formatting | bytes 8388608
  155.0 0.0 copy-done
  155.0 1.0 copy.12
Async XLA Ops:
  150.3 4.7 %copy-start = (f32[1,256,1024]{2,1,0:T(8,128)S(1)}, f32[1,256,1024]{2,1,0:T(8,128)}, u32[]{:S(2)}) copy-start(f32[1,256,1024]{2,1,0:T(8,128)} %get-tuple-element.5) | copy-start | bytes 3145732

commit v3 on v2

--- a/solution.py
+++ b/solution.py
@@ -42,8 +42,8 @@
     U, C,
     panel, diag, dinv, uf, vf, keep, sketch,
     out, diag_out,
-    t0f, t0b, tc, bf, f, r, r_rx, basis, xp, x_rx, e, acc, near, near_rx, far, far_rx,
-    t_s, t_r, bx_s, bx_r, f_s, f_r, r_s, r_r, b_s, b_r, x_s, x_r, e_s, e_r,
+    t0f, t0b, tx, tc, bf, pair, f, r, r_rx, basis, xp, x_rx, e, acc, near, near_rx, far, far_rx,
+    g_s, g_r, t_s, t_r, bx_s, bx_r, f_s, f_r, r_s, r_r, b_s, b_r, x_s, x_r, e_s, e_r,
     near_s, near_r, far_s, far_r,
 ):
     M, RD, B = panel.shape[1:]
@@ -94,44 +94,79 @@
             for v in range(U):
                 greet(v, me_c - m - 1)
 
+    pl.semaphore_wait(
+        barrier, U - 1 + U * (jnp.minimum(M, C - 1 - me_c) + jnp.minimum(M, me_c))
+    )
+
+    def scatter_out(buf, k, land, send, recv):
+        return copy(
+            buf.at[tiles(after(k))], land.at[k - 1], send.at[k - 1], recv.at[k - 1], after(k), me_c
+        )
+
+    def rows_of(u):
+        return pl.ds(pl.multiple_of(u * RD, RD), RD)
+
+    sends = jnp.minimum(M, C - 1 - me_c)
+
+    def tile(n):
+        return lax.rem(sends - 1 - n + M, M)
+
+    def g_copy(m, k):
+        return copy(
+            t0b.at[m, after(k)], tx.at[m, rows_of(me_u)],
+            g_s.at[m, k - 1], g_r.at[m, k - 1], after(k), me_c,
+        )
+
+    def t_copy(m):
+        return copy(
+            tx.at[m], tc.at[:, pl.ds(pl.multiple_of(m * CB, CB), CB)],
+            t_s.at[m], t_r.at[m], me_u, to_column(m),
+        )
+
+    def solve(first, last):
+        @pl.loop(first, last)
+        def _(n):
+            m = tile(n)
+            for v in range(U):
+                block = dot(panel[0, m], dinv[0, v * CB : (v + 1) * CB, :], NT)
+                t0f[m, :, v * CB : (v + 1) * CB] = block
+                t0b[m, v] = block.astype(BF16)
+
+            @pl.when(n < sends)
+            def _():
+                for k in range(1, U):
+                    g_copy(m, k).start()
+                tx[m, rows_of(me_u), :] = t0b[m, me_u]
+
+    def forward(first, last):
+        @pl.loop(first, last)
+        def _(n):
+            @pl.when(n < sends)
+            def _():
+                m = tile(n)
+                for k in range(1, U):
+                    region = tx.at[m, rows_of(before(k))]
+                    copy(
+                        region, region, g_s.at[m, k - 1], g_r.at[m, k - 1], after(k), me_c
+                    ).wait_recv()
+                t_copy(m).start()
+
+    solve(0, min(2, M))
+
     @pl.loop(0, M)
     def _(t):
         probe = (dot(sketch[0], vf[0, t, 0], NT) * keep[t]).astype(BF16)
         r[t] = dot(probe, uf[0, t, 0], NN).astype(BF16)
 
-    pl.semaphore_wait(
-        barrier, U - 1 + U * (jnp.minimum(M, C - 1 - me_c) + jnp.minimum(M, me_c))
-    )
-
-    def scatter_out(buf, k, land, send, recv):
-        return copy(
-            buf.at[tiles(after(k))], land.at[k - 1], send.at[k - 1], recv.at[k - 1], after(k), me_c
-        )
-
     for k in range(1, U):
         scatter_out(r, k, r_rx, r_s, r_r).start()
 
-    def t_copy(m, v):
-        return copy(
-            t0b.at[m, v],
-            tc.at[pl.ds(me_u * RD, RD), pl.ds(pl.multiple_of(m * CB, CB), CB)],
-            t_s.at[m, v], t_r.at[m, me_u], v, to_column(m),
-        )
-
-    @pl.loop(0, M)
-    def _(m):
-        for v in range(U):
-            block = dot(panel[0, m], dinv[0, v * CB : (v + 1) * CB, :], NT)
-            t0f[m, :, v * CB : (v + 1) * CB] = block
-            t0b[m, v] = block.astype(BF16)
-
-        @pl.when(to_column(m) < C)
-        def _():
-            for v in range(U):
-                t_copy(m, v).start()
+    solve(min(2, M), M)
+    forward(0, min(2, M))
 
     for k in range(1, U):
         scatter_out(r, k, r_rx, r_s, r_r).wait_recv()
+    forward(min(2, M), min(4, M))
 
     summed = r[own].astype(F32)
     for k in range(1, U):
@@ -169,6 +204,7 @@
         def _():
             b_copy(i).start()
 
+    forward(min(4, M), M)
     for k in range(1, U):
         gather_in(basis, k, b_s, b_r).wait_recv()
 
@@ -231,19 +267,11 @@
 
         @pl.when(me_c - m - 1 >= 0)
         def _():
-            @pl.loop(0, U)
-            def _(s):
-                copy(
-                    t0b.at[m, 0], tc.at[pl.ds(s * RD, RD), cols],
-                    t_s.at[m, 0], t_r.at[m, s], me_u, me_c,
-                ).wait_recv()
+            t_copy(m).wait_recv()
 
         @pl.when(me_c - m - 1 < 0)
         def _():
             tc[:, cols] = jnp.zeros((B, CB), BF16)
-
-    def rows_of(u):
-        return pl.ds(pl.multiple_of(u * RD, RD), RD)
 
     @pl.loop(0, U)
     def _(u):
@@ -265,12 +293,13 @@
         def _():
             bf[i] = jnp.zeros((2, K, B), BF16)
 
+    for i in range(MT):
+        for n in range(2):
+            pair[i, n] = bf[i, 1 - n]
+
     def product(u):
-        total = acc[rows_of(u), :]
-        for i in range(MT):
-            total = total - dot(bf[i, 0, :, rows_of(u)], bf[i, 1], TN)
-            total = total - dot(bf[i, 1, :, rows_of(u)], bf[i, 0], TN)
-        return total
+        left = bf[:, :, :, rows_of(u)].reshape(2 * MT * K, RD)
+        return acc[rows_of(u), :] - dot(left, pair[...].reshape(2 * MT * K, B), TN)
 
     X = U // 2
     side = lax.rem(me_u, 2)
@@ -321,8 +350,9 @@
     def _(m):
         @pl.when(to_column(m) < C)
         def _():
-            for v in range(U):
-                t_copy(m, v).wait_send()
+            for k in range(1, U):
+                g_copy(m, k).wait_send()
+            t_copy(m).wait_send()
             f_copy(m, lax.rem(m, MT)).wait_send()
 
 
@@ -347,7 +377,9 @@
         scratch_shapes=[
             pltpu.VMEM((M, RD, B), F32),
             pltpu.VMEM((M, U, RD, CB), BF16),
+            pltpu.VMEM((M, B, CB), BF16),
             pltpu.VMEM((B, M * CB), BF16),
+            pltpu.VMEM((MT, 2, K, B), BF16),
             pltpu.VMEM((MT, 2, K, B), BF16),
             pltpu.VMEM((M, K, RD), BF16),
             pltpu.VMEM((M, K, B), BF16),
@@ -361,7 +393,7 @@
             pltpu.VMEM((X, RD, B), BF16),
             pltpu.VMEM((X - 1, RD, B), BF16),
             pltpu.VMEM((X - 1, RD, B), BF16),
-            dma((M, U)), dma((M, U)), dma((MT,)), dma((MT,)), dma((M,)), dma((MT, U)),
+            dma((M, U - 1)), dma((M, U - 1)), dma((M,)), dma((M,)), dma((MT,)), dma((MT,)), dma((M,)), dma((MT, U)),
             *peers, *peers, *peers, *peers,
             dma((X,)), dma((X,)), dma((X - 1,)), dma((X - 1,)),
         ],

time: 156 us -> 148 us (0.949)
  Pallas kernels: 148 us -> 139 us
    pallas_call x1, Pallas kernels: 148 us -> 139 us  [local(): pl.pallas_call(functools.partial(kernel, U, C), out_shape=(jax.ShapeDtype...]
where the time goes in v3:
time: 148 us; the launch traced here: 147 us
  Pallas kernels  139 us (94%)
  local copies, waits for them, and re-layouts  5.7 us (4%)
    pallas_call x1, Pallas kernels, local(): pl.pallas_call(functools.partial(kernel, U, C), out_shape=(jax.ShapeDtype...  139 us
    unnamed x4, local copies, waits for them, and re-layouts  5.7 us

profile of v3, /device:TPU:29, one launch (start us, length us, event | category | flops | bytes accessed | tf_op | source)
XLA Modules:
  0.0 147.0 jit_solution(3510631007868289344)
XLA Ops:
  0.6 1.3 compare_convert_fusion.keep
  2.0 139.3 %band_window.1 = (bf16[1,8,256,1024]{3,2,1,0:T(8,128)(2,1)}, f32[1,256,1024]{2,1,0:T(8,128)}) custom-call(bf16[1,8,256,1024]{3,2,1,0:T(8,128)(2,1)} %panel.1, bf16[1,256,1024]{2,1,0:T(8,128)(2,1)} %diag.1, bf16[1,1024,1024]{2,1,0:T(8,128)(2,1)} %dinv.1, bf16[1,8,1,96,1024]{4,3,2,1,0:T(8,128)(2,1)} %uf.1, bf16[1,8,1,96,1024]{4,3,2,1,0:T(8,128)(2,1)} %vf.1, ...), custom_call_target="tpu_custom_call" | custom-call | tf_op jit(solution)/shard_map/band_window/pallas_call | solution.py:369
  141.3 0.0 copy-start
  141.3 4.7 %copy.11 = bf16[1,8,256,1024]{3,2,1,0:T(8,128)(2,1)} copy(bf16[1,8,256,1024]{3,2,1,0:T(8,128)(2,1)} %get-tuple-element.4) | data formatting | bytes 8388608
  146.0 0.0 copy-done
  146.0 1.0 copy.12
Async XLA Ops:
  141.3 4.7 %copy-start = (f32[1,256,1024]{2,1,0:T(8,128)S(1)}, f32[1,256,1024]{2,1,0:T(8,128)}, u32[]{:S(2)}) copy-start(f32[1,256,1024]{2,1,0:T(8,128)} %get-tuple-element.5) | copy-start | bytes 3145732
